TPU v7x, 32 devices: a whole 2x2x4 slice. The times are simulated.
32 devices in a mesh: shots: 2 (over x), gx: 16 (over z, y, core).
Axes of the slice: x: 2, y: 2, z: 4, core: 2. Of those that a mesh axis runs over, the one named last changes fastest.
Arguments:
- courant_sq: float32 [128, 128, 128], P('gx'), may hold values from 0.03 to 0.2
- wave_prev: float32 [256, 128, 128], P(('shots', 'gx')), parts along dimension 0, may hold values from -6 to 6
- wave_now: float32 [256, 128, 128], P(('shots', 'gx')), parts along dimension 0, may hold values from -6 to 6
- adj_late: float32 [256, 128, 128], P(('shots', 'gx')), parts along dimension 0, may hold values from -6 to 6
- adj_last: float32 [256, 128, 128], P(('shots', 'gx')), parts along dimension 0, may hold values from -6 to 6
- wavelet: float32 [24], P('shots'), parts along dimension 0, may hold values from -48 to 48
- source_cell: int32 [2], P('shots'), parts along dimension 0, may hold values from 0 to 2097151
- receivers: int32 [2048], P('shots'), parts along dimension 0, may hold values from 0 to 2097151
- observed: float32 [24, 1024], P('shots'), parts along dimension 0, may hold values from -6 to 6
- footprint: int32 [4096], P(('shots', 'gx')), parts along dimension 0, may hold values 0 or 1
- brick_owner: int32 [2048, 1], P('gx'), may hold values from 0 to 15; in each aligned block of 128 rows (0 to 127, 128 to 255, ...) at most 16 rows name the same one
- prior_in: bfloat16 [32, 27], replicated, may hold values from -1.25 to 1.25
- prior_in_bias: float32 [32], replicated, may hold values from -3 to 3
- prior_mix: bfloat16 [32, 32], replicated, may hold values from -1 to 1
- prior_mix_bias: float32 [32], replicated, may hold values from -3 to 3
- prior_out: bfloat16 [27, 32], replicated, may hold values from -0.21875 to 0.21875
- prior_out_bias: float32 [1], replicated, may hold values from -3 to 3
Outputs:
- residual_traces: float32 [24, 1024], P('shots'), parts along dimension 0
- owned_bricks: bfloat16 [32, 16, 16, 1024], P(('shots', 'gx')), parts along dimension 0
There are 2 independent parts, one for each index of `shots`. A program takes and returns all parts, laid end to end along the dimension named above; an argument that names none is the same for every part. Nothing has to cross between parts.
Inputs may be any that keep to these rules, and one draw needn't show every extreme that they name: `brick_owner`: among the 128 bricks of one device's block, at most 16 have the same owner.
All inputs are finite; a program needn't handle non-finite values. No bound on the sum of `footprint` on one device may be relied on, other than what follows from the above.
Results may differ from a plain program's by a relative error of at most 0.0045.
Values may be sent and summed in bfloat16 or wider, within the bound.
A program may use at most 128 MiB of HBM per device.

v0:
```python
import jax
import jax.numpy as jnp
from jax import lax
from jax.sharding import PartitionSpec as P

OFFSETS = [(a, b, c) for a in range(3) for b in range(3) for c in range(3)]


def padded_2(cells, sides, width):
    for axis, dim in sides:
        count = lax.axis_size(axis)
        ends = count - 1
        head = lax.slice_in_dim(cells, 0, width, axis=dim)
        tail = lax.slice_in_dim(cells, cells.shape[dim] - width, cells.shape[dim], axis=dim)
        cells = jnp.concatenate(
            [
                lax.ppermute(tail, axis, [(i, (i + 1) % count) for i in range(ends)]),
                cells,
                lax.ppermute(head, axis, [((i + 1) % count, i) for i in range(ends)]),
            ],
            axis=dim,
        )
    return cells


def laplace(widened):
    inner = widened[2:-2]
    along_x = 16.0 * (widened[3:-1] + widened[1:-3]) - (widened[4:] + widened[:-4])
    pad_y = jnp.pad(inner, ((0, 0), (2, 2), (0, 0)))
    along_y = 16.0 * (pad_y[:, 3:-1] + pad_y[:, 1:-3]) - (pad_y[:, 4:] + pad_y[:, :-4])
    pad_z = jnp.pad(inner, ((0, 0), (0, 0), (2, 2)))
    along_z = 16.0 * (pad_z[:, :, 3:-1] + pad_z[:, :, 1:-3]) - (pad_z[:, :, 4:] + pad_z[:, :, :-4])
    return (along_x + along_y + along_z - 90.0 * inner) / 12.0


def leapfrog(before, widened, coeffs):
    return 2.0 * widened[2:-2] - before + coeffs * laplace(widened)


def inject(field, base_x, cells, values):
    plane = field.shape[1] * field.shape[2]
    count = field.shape[0] * plane
    relative = cells - base_x * plane
    inside = (relative >= 0) & (relative < count)
    clipped = jnp.clip(relative, 0, count - 1)
    flattened = field.reshape(-1).at[clipped].add(jnp.where(inside, values, 0.0))
    return flattened.reshape(field.shape)


def sample(field, base_x, cells):
    plane = field.shape[1] * field.shape[2]
    count = field.shape[0] * plane
    relative = cells - base_x * plane
    inside = (relative >= 0) & (relative < count)
    clipped = jnp.clip(relative, 0, count - 1)
    return jnp.where(inside, field.reshape(-1)[clipped], 0.0)


def lifting(widened, weight_in, bias_in, weight_mix, bias_mix):
    planes = widened.shape[0] - 2
    rows_y = widened.shape[1]
    rows_z = widened.shape[2]
    padded = jnp.pad(widened, ((0, 0), (1, 1), (1, 1)))
    stacked = jnp.stack(
        [padded[a : a + planes, b : b + rows_y, c : c + rows_z] for a, b, c in OFFSETS]
    ).reshape(27, -1)
    lifted = jnp.dot(weight_in, stacked, preferred_element_type=jnp.float32) + bias_in[:, None]
    lifted = jnp.maximum(lifted, 0.0).astype(jnp.bfloat16)
    hidden = jnp.dot(weight_mix, lifted, preferred_element_type=jnp.float32) + bias_mix[:, None]
    return jnp.maximum(hidden, 0.0).astype(jnp.bfloat16).reshape(-1, planes, rows_y, rows_z)


def project(widened, weight_out, bias_out):
    channels = widened.shape[0]
    planes = widened.shape[1] - 2
    rows_y = widened.shape[2]
    rows_z = widened.shape[3]
    products = jnp.dot(
        weight_out, widened.reshape(channels, -1), preferred_element_type=jnp.float32
    )
    products = jnp.pad(
        products.reshape(27, planes + 2, rows_y, rows_z), ((0, 0), (0, 0), (1, 1), (1, 1))
    )
    summed = jnp.zeros((planes, rows_y, rows_z), jnp.float32)
    for position, (a, b, c) in enumerate(OFFSETS):
        summed = summed + products[position, a : a + planes, b : b + rows_y, c : c + rows_z]
    return summed + bias_out[0]


def rim_one(field):
    return padded_2(field, (("gx", 0),), 2)


def per_device(
    courant_sq,
    wave_prev,
    wave_now,
    adj_late,
    adj_last,
    wavelet,
    source_cell,
    receivers,
    observed,
    footprint,
    brick_owner,
    prior_in,
    prior_in_bias,
    prior_mix,
    prior_mix_bias,
    prior_out,
    prior_out_bias,
):
    cells_x, cells_y, cells_z = wave_now.shape
    devices = lax.axis_size("gx")
    anchor = lax.axis_index("gx") * cells_x
    total_x = cells_x * devices
    field_shape = wave_now.shape

    def forward_step(loop_state, impulse):
        before, current = loop_state
        newest = inject(
            leapfrog(before, rim_one(current), courant_sq), anchor, source_cell, impulse[None]
        )
        return (
            (current, newest),
            (newest - 2.0 * current + before, sample(newest, anchor, receivers)),
        )

    _, (changes, records) = lax.scan(forward_step, (wave_prev, wave_now), wavelet)
    residual_traces = lax.psum(records, "gx") - observed
    zeros_field = jnp.zeros(field_shape, jnp.float32)

    def adjoint_step(loop_state, inputs):
        future, current, summed = loop_state
        misfit, change = inputs
        newest = inject(leapfrog(future, rim_one(current), courant_sq), anchor, receivers, misfit)
        return ((current, newest, summed + newest * change), None)

    (_, _, grad), _ = lax.scan(
        adjoint_step, (adj_late, adj_last, zeros_field), (residual_traces[::-1], changes[::-1])
    )
    grad_low = grad.astype(jnp.bfloat16)
    grad_wide = padded_2(grad_low, (("gx", 0),), 2)
    hidden = lifting(grad_wide, prior_in, prior_in_bias, prior_mix, prior_mix_bias)
    margin = anchor - 1 + jnp.arange(cells_x + 2, dtype=jnp.int32)
    keep = ((margin >= 0) & (margin < total_x))[None, :, None, None]
    hidden_wide = jnp.where(keep, hidden, jnp.zeros_like(hidden))
    conv = project(hidden_wide, prior_out, prior_out_bias)
    model_grad = (grad + conv).astype(jnp.bfloat16)
    bricks = model_grad.transpose(1, 0, 2).reshape(cells_y, cells_x * cells_z)
    bricks = jnp.where((footprint == 1)[:, None], bricks, jnp.zeros_like(bricks))
    owners = brick_owner[:, 0]
    same = owners[:, None] == owners[None, :]
    lower = (
        jnp.arange(cells_y, dtype=jnp.int32)[:, None]
        > jnp.arange(cells_y, dtype=jnp.int32)[None, :]
    )
    slots = jnp.sum((same & lower).astype(jnp.int32), axis=1)
    capacity = max(2, 2 * cells_y // devices)
    buckets = (
        jnp.zeros((devices, capacity, cells_x * cells_z), jnp.bfloat16)
        .at[owners, slots]
        .set(bricks)
    )
    arrived = lax.all_to_all(buckets, "gx", split_axis=0, concat_axis=0, tiled=True)
    return (residual_traces, arrived[None])


def solution(mesh):
    return jax.shard_map(
        per_device,
        mesh=mesh,
        in_specs=(
            P("gx", None, None),
            P(("shots", "gx"), None, None),
            P(("shots", "gx"), None, None),
            P(("shots", "gx"), None, None),
            P(("shots", "gx"), None, None),
            P("shots"),
            P("shots"),
            P("shots"),
            P("shots", None),
            P(("shots", "gx")),
            P("gx", None),
            P(),
            P(),
            P(),
            P(),
            P(),
            P(),
        ),
        out_specs=(P("shots", None), P(("shots", "gx"), None, None, None)),
        check_vma=False,
    )
```

profile of v0, /device:TPU:11, one launch (start us, length us, event | category | flops | bytes accessed | tf_op | source)
XLA Modules:
  0.0 700.3 jit_solution(2389430900600771791)
XLA Ops:
  3.5 228.7 %while.36 = (s32[]{:T(128)}, f32[8,128,128]{2,1,0:T(8,128)S(1)}, f32[8,128,128]{2,1,0:T(8,128)S(1)}, f32[12,8,128,128]{3,2,1,0:T(8,128)}, f32[12,1024]{1,0:T(8,1...) while((s32[]{:T(128)}, f32[8,128,128]{2,1,0:T(8,128)S(1)}, ...), condition=%wide.region_1.2_spmd, body=%wide.region_0.1_spmd.sunk | while | flops 3156997 | bytes 12133655 | solution.py:129
  232.2 45.2 %psum.7 = f32[12,1024]{1,0:T(8,128)S(1)} all-reduce(f32[12,1024]{1,0:T(8,128)S(1)} %get-tuple-element.278), channel_id=1, replica_groups=mesh['shots'=2,'gx'=16] {'gx'}, use_global_device_ids=true, to_apply=%region_2.3 | all-reduce | flops 12288 | bytes 98304 | tf_op jit(solution)/shard_map/psum | solution.py:130
  283.9 220.2 %while.37 = (s32[]{:T(128)}, f32[8,128,128]{2,1,0:T(8,128)S(1)}, f32[8,128,128]{2,1,0:T(8,128)S(1)}, f32[8,128,128]{2,1,0:T(8,128)S(1)}, f32[8,128,128]{2,1,0:T(...) while((s32[]{:T(128)}, f32[8,128,128]{2,1,0:T(8,128)S(1)}, ...), condition=%wide.region_6.7_spmd.clone, body=%wide.region_4.6_spmd.clone.sunk | while | flops 3156995 | bytes 12112095 | solution.py:139
  294.6 6.4 scatter_fusion
  312.3 6.4 scatter_fusion
  322.1 6.6 collective-permute-start.3
  330.4 6.4 scatter_fusion
  340.2 6.5 collective-permute-start.3
  348.5 6.4 scatter_fusion
  358.3 6.5 collective-permute-start.3
  369.0 6.4 scatter_fusion
  387.2 6.4 scatter_fusion
  405.4 6.4 scatter_fusion
  423.7 6.4 scatter_fusion
  441.9 6.4 scatter_fusion
  460.1 6.4 scatter_fusion
  478.2 6.4 scatter_fusion
  563.7 54.1 %stack.111 = bf16[27,163840]{1,0:T(8,128)(2,1)} concatenate(bf16[1,163840]{1,0:T(2,128)(2,1)} %stack.84, bf16[1,163840]{1,0:T(2,128)(2,1)} %stack.85, bf16[1,163840]{1,0:T(2,128)(2,1)} %stack.86, bf16[1,163840]{1,0:T(2,128)(2,1)} %stack.87, bf16[1,163840]{1,0:T(2,128)(2,1)S(1)} %stack.88, bf16[1,163840]{1,0:T(2,128)(2,1)} %stack.89, bf16[1,163840]{1,0:T(2,128)(2,1)} %stack.90, ...), dimensions={0} | concatenate | bytes 17694720 | tf_op jit(solution)/shard_map/stack | solution.py:64
  617.9 10.8 %fusion.31 = bf16[163840,32]{0,1:T(8,128)(2,1)} fusion(bf16[27,163840]{1,0:T(8,128)(2,1)} %stack.111, bf16[32,27]{1,0:T(8,128)(2,1)S(1)} %copy-done, f32[32]{0:T(128)S(1)} %copy-done.12), kind=kOutput, calls=%fused_computation.95 | convolution fusion | flops 298844160 | bytes 19334976 | tf_op jit(solution)/shard_map/dot_general | solution.py:67
  628.9 12.7 %fusion.35 = f32[163840,27]{0,1:T(8,128)} fusion(bf16[27,32]{1,0:T(8,128)(2,1)S(1)} %copy-done.10, bf16[32,32]{1,0:T(8,128)(2,1)S(1)} %copy-done.9, bf16[163840,32]{0,1:T(8,128)(2,1)} %fusion.31, f32[32]{0:T(128)S(1)} %copy-done.11, pred[163840]{0:T(1024)(128)(4,1)S(1)} %bitcast.208), kind=kOutput, calls=%fused_computation.99 | convolution fusion | flops 639631360 | bytes 28348224 | tf_op jit(solution)/shard_map/dot_general | solution.py:78
  641.6 19.2 %copy.23 = f32[4,8,1280,128]{3,2,1,0:T(8,128)} copy(f32[4,8,1280,128]{3,1,2,0:T(8,128)} %bitcast.204) | data formatting | bytes 41943040
  660.9 7.1 %slice.443 = f32[27,1280,128]{2,1,0:T(8,128)S(1)} slice(f32[32,1280,128]{2,1,0:T(8,128)} %bitcast.206), slice={[0:27], [0:1280], [0:128]} | slice | bytes 35389440
  670.5 9.0 %scatter_fusion.1 = bf16[16,16,1024]{2,1,0:T(8,128)(2,1)S(1)} fusion(bf16[16,16,1024]{2,1,0:T(8,128)(2,1)S(1)} %broadcast_in_dim.77, s32[128]{0:T(128)S(1)} %fusion.78, bf16[128,1024]{1,0:T(8,128)(2,1)S(1)} %bitcast_select_fusion), kind=kCustom, calls=%fused_computation.2 | custom fusion | bytes 787456 | tf_op jit(solution)/shard_map/scatter | solution.py:163
  679.5 20.0 %all_to_all.5 = bf16[16,16,1024]{2,1,0:T(8,128)(2,1)S(1)} all-to-all(bf16[16,16,1024]{2,1,0:T(8,128)(2,1)S(1)} %scatter_fusion.1), channel_id=1, replica_groups=mesh['shots'=2,'gx'=16] {'gx'}, dimensions={0} | all-to-all | bytes 1048576 | tf_op jit(solution)/shard_map/all_to_all | solution.py:165
  (523 shorter events, 426.5 us)
Async XLA Ops:
  44.2 7.2 %collective-permute-start.1 = (f32[2,128,128]{2,1,0:T(8,128)S(1)}, f32[2,128,128]{2,1,0:T(8,128)S(1)}, u32[]{:S(2)}, u32[]{:S(2)}) collective-permute-start(f32[2,128,128]{2,1,0:T(8,128)S(1)} %get-tuple-element.520), channel_id=1, source_target_pairs={{1,0},{2,1},{3,2},{4,3},{5,4},{6,5},{7,6},{8,7},{9,8},{10,9},{11,1... | collective-permute-start | bytes 393224 | tf_op jit(solution)/shard_map/while/body/eval_jaxpr/ppermute | solution.py:19
  63.2 7.2 %collective-permute-start.1 = (f32[2,128,128]{2,1,0:T(8,128)S(1)}, f32[2,128,128]{2,1,0:T(8,128)S(1)}, u32[]{:S(2)}, u32[]{:S(2)}) collective-permute-start(f32[2,128,128]{2,1,0:T(8,128)S(1)} %get-tuple-element.520), channel_id=1, source_target_pairs={{1,0},{2,1},{3,2},{4,3},{5,4},{6,5},{7,6},{8,7},{9,8},{10,9},{11,1... | collective-permute-start | bytes 393224 | tf_op jit(solution)/shard_map/while/body/eval_jaxpr/ppermute | solution.py:19
  82.2 7.2 %collective-permute-start.1 = (f32[2,128,128]{2,1,0:T(8,128)S(1)}, f32[2,128,128]{2,1,0:T(8,128)S(1)}, u32[]{:S(2)}, u32[]{:S(2)}) collective-permute-start(f32[2,128,128]{2,1,0:T(8,128)S(1)} %get-tuple-element.520), channel_id=1, source_target_pairs={{1,0},{2,1},{3,2},{4,3},{5,4},{6,5},{7,6},{8,7},{9,8},{10,9},{11,1... | collective-permute-start | bytes 393224 | tf_op jit(solution)/shard_map/while/body/eval_jaxpr/ppermute | solution.py:19
  101.2 7.2 %collective-permute-start.1 = (f32[2,128,128]{2,1,0:T(8,128)S(1)}, f32[2,128,128]{2,1,0:T(8,128)S(1)}, u32[]{:S(2)}, u32[]{:S(2)}) collective-permute-start(f32[2,128,128]{2,1,0:T(8,128)S(1)} %get-tuple-element.520), channel_id=1, source_target_pairs={{1,0},{2,1},{3,2},{4,3},{5,4},{6,5},{7,6},{8,7},{9,8},{10,9},{11,1... | collective-permute-start | bytes 393224 | tf_op jit(solution)/shard_map/while/body/eval_jaxpr/ppermute | solution.py:19
  120.2 7.2 %collective-permute-start.1 = (f32[2,128,128]{2,1,0:T(8,128)S(1)}, f32[2,128,128]{2,1,0:T(8,128)S(1)}, u32[]{:S(2)}, u32[]{:S(2)}) collective-permute-start(f32[2,128,128]{2,1,0:T(8,128)S(1)} %get-tuple-element.520), channel_id=1, source_target_pairs={{1,0},{2,1},{3,2},{4,3},{5,4},{6,5},{7,6},{8,7},{9,8},{10,9},{11,1... | collective-permute-start | bytes 393224 | tf_op jit(solution)/shard_map/while/body/eval_jaxpr/ppermute | solution.py:19
  139.2 7.2 %collective-permute-start.1 = (f32[2,128,128]{2,1,0:T(8,128)S(1)}, f32[2,128,128]{2,1,0:T(8,128)S(1)}, u32[]{:S(2)}, u32[]{:S(2)}) collective-permute-start(f32[2,128,128]{2,1,0:T(8,128)S(1)} %get-tuple-element.520), channel_id=1, source_target_pairs={{1,0},{2,1},{3,2},{4,3},{5,4},{6,5},{7,6},{8,7},{9,8},{10,9},{11,1... | collective-permute-start | bytes 393224 | tf_op jit(solution)/shard_map/while/body/eval_jaxpr/ppermute | solution.py:19
  158.2 7.2 %collective-permute-start.1 = (f32[2,128,128]{2,1,0:T(8,128)S(1)}, f32[2,128,128]{2,1,0:T(8,128)S(1)}, u32[]{:S(2)}, u32[]{:S(2)}) collective-permute-start(f32[2,128,128]{2,1,0:T(8,128)S(1)} %get-tuple-element.520), channel_id=1, source_target_pairs={{1,0},{2,1},{3,2},{4,3},{5,4},{6,5},{7,6},{8,7},{9,8},{10,9},{11,1... | collective-permute-start | bytes 393224 | tf_op jit(solution)/shard_map/while/body/eval_jaxpr/ppermute | solution.py:19
  177.2 7.2 %collective-permute-start.1 = (f32[2,128,128]{2,1,0:T(8,128)S(1)}, f32[2,128,128]{2,1,0:T(8,128)S(1)}, u32[]{:S(2)}, u32[]{:S(2)}) collective-permute-start(f32[2,128,128]{2,1,0:T(8,128)S(1)} %get-tuple-element.520), channel_id=1, source_target_pairs={{1,0},{2,1},{3,2},{4,3},{5,4},{6,5},{7,6},{8,7},{9,8},{10,9},{11,1... | collective-permute-start | bytes 393224 | tf_op jit(solution)/shard_map/while/body/eval_jaxpr/ppermute | solution.py:19
  215.1 7.2 %collective-permute-start.1 = (f32[2,128,128]{2,1,0:T(8,128)S(1)}, f32[2,128,128]{2,1,0:T(8,128)S(1)}, u32[]{:S(2)}, u32[]{:S(2)}) collective-permute-start(f32[2,128,128]{2,1,0:T(8,128)S(1)} %get-tuple-element.520), channel_id=1, source_target_pairs={{1,0},{2,1},{3,2},{4,3},{5,4},{6,5},{7,6},{8,7},{9,8},{10,9},{11,1... | collective-permute-start | bytes 393224 | tf_op jit(solution)/shard_map/while/body/eval_jaxpr/ppermute | solution.py:19
  284.0 9.0 %collective-permute-start.2 = (f32[2,128,128]{2,1,0:T(8,128)S(1)}, f32[2,128,128]{2,1,0:T(8,128)S(1)}, u32[]{:S(2)}, u32[]{:S(2)}) collective-permute-start(f32[2,128,128]{2,1,0:T(8,128)S(1)} %get-tuple-element.530), channel_id=1, source_target_pairs={{0,1},{1,2},{2,3},{3,4},{4,5},{5,6},{6,7},{7,8},{8,9},{9,10},{10,1... | collective-permute-start | bytes 393224 | tf_op jit(solution)/shard_map/while/body/eval_jaxpr/ppermute | solution.py:17
  302.5 8.1 %collective-permute-start.2 = (f32[2,128,128]{2,1,0:T(8,128)S(1)}, f32[2,128,128]{2,1,0:T(8,128)S(1)}, u32[]{:S(2)}, u32[]{:S(2)}) collective-permute-start(f32[2,128,128]{2,1,0:T(8,128)S(1)} %get-tuple-element.530), channel_id=1, source_target_pairs={{0,1},{1,2},{2,3},{3,4},{4,5},{5,6},{6,7},{7,8},{8,9},{9,10},{10,1... | collective-permute-start | bytes 393224 | tf_op jit(solution)/shard_map/while/body/eval_jaxpr/ppermute | solution.py:17
  320.1 8.6 %collective-permute-start.2 = (f32[2,128,128]{2,1,0:T(8,128)S(1)}, f32[2,128,128]{2,1,0:T(8,128)S(1)}, u32[]{:S(2)}, u32[]{:S(2)}) collective-permute-start(f32[2,128,128]{2,1,0:T(8,128)S(1)} %get-tuple-element.530), channel_id=1, source_target_pairs={{0,1},{1,2},{2,3},{3,4},{4,5},{5,6},{6,7},{7,8},{8,9},{9,10},{10,1... | collective-permute-start | bytes 393224 | tf_op jit(solution)/shard_map/while/body/eval_jaxpr/ppermute | solution.py:17
  322.1 7.6 %collective-permute-start.3 = (f32[2,128,128]{2,1,0:T(8,128)S(1)}, f32[2,128,128]{2,1,0:T(8,128)S(1)}, u32[]{:S(2)}, u32[]{:S(2)}) collective-permute-start(f32[2,128,128]{2,1,0:T(8,128)S(1)} %get-tuple-element.533), channel_id=1, source_target_pairs={{1,0},{2,1},{3,2},{4,3},{5,4},{6,5},{7,6},{8,7},{9,8},{10,9},{11,1... | collective-permute-start | bytes 393224 | tf_op jit(solution)/shard_map/while/body/eval_jaxpr/ppermute | solution.py:19
  338.3 8.5 %collective-permute-start.2 = (f32[2,128,128]{2,1,0:T(8,128)S(1)}, f32[2,128,128]{2,1,0:T(8,128)S(1)}, u32[]{:S(2)}, u32[]{:S(2)}) collective-permute-start(f32[2,128,128]{2,1,0:T(8,128)S(1)} %get-tuple-element.530), channel_id=1, source_target_pairs={{0,1},{1,2},{2,3},{3,4},{4,5},{5,6},{6,7},{7,8},{8,9},{9,10},{10,1... | collective-permute-start | bytes 393224 | tf_op jit(solution)/shard_map/while/body/eval_jaxpr/ppermute | solution.py:17
  340.2 7.5 %collective-permute-start.3 = (f32[2,128,128]{2,1,0:T(8,128)S(1)}, f32[2,128,128]{2,1,0:T(8,128)S(1)}, u32[]{:S(2)}, u32[]{:S(2)}) collective-permute-start(f32[2,128,128]{2,1,0:T(8,128)S(1)} %get-tuple-element.533), channel_id=1, source_target_pairs={{1,0},{2,1},{3,2},{4,3},{5,4},{6,5},{7,6},{8,7},{9,8},{10,9},{11,1... | collective-permute-start | bytes 393224 | tf_op jit(solution)/shard_map/while/body/eval_jaxpr/ppermute | solution.py:19
  356.3 8.5 %collective-permute-start.2 = (f32[2,128,128]{2,1,0:T(8,128)S(1)}, f32[2,128,128]{2,1,0:T(8,128)S(1)}, u32[]{:S(2)}, u32[]{:S(2)}) collective-permute-start(f32[2,128,128]{2,1,0:T(8,128)S(1)} %get-tuple-element.530), channel_id=1, source_target_pairs={{0,1},{1,2},{2,3},{3,4},{4,5},{5,6},{6,7},{7,8},{8,9},{9,10},{10,1... | collective-permute-start | bytes 393224 | tf_op jit(solution)/shard_map/while/body/eval_jaxpr/ppermute | solution.py:17
  358.3 10.0 %collective-permute-start.3 = (f32[2,128,128]{2,1,0:T(8,128)S(1)}, f32[2,128,128]{2,1,0:T(8,128)S(1)}, u32[]{:S(2)}, u32[]{:S(2)}) collective-permute-start(f32[2,128,128]{2,1,0:T(8,128)S(1)} %get-tuple-element.533), channel_id=1, source_target_pairs={{1,0},{2,1},{3,2},{4,3},{5,4},{6,5},{7,6},{8,7},{9,8},{10,9},{11,1... | collective-permute-start | bytes 393224 | tf_op jit(solution)/shard_map/while/body/eval_jaxpr/ppermute | solution.py:19
  378.8 7.7 %collective-permute-start.3 = (f32[2,128,128]{2,1,0:T(8,128)S(1)}, f32[2,128,128]{2,1,0:T(8,128)S(1)}, u32[]{:S(2)}, u32[]{:S(2)}) collective-permute-start(f32[2,128,128]{2,1,0:T(8,128)S(1)} %get-tuple-element.533), channel_id=1, source_target_pairs={{1,0},{2,1},{3,2},{4,3},{5,4},{6,5},{7,6},{8,7},{9,8},{10,9},{11,1... | collective-permute-start | bytes 393224 | tf_op jit(solution)/shard_map/while/body/eval_jaxpr/ppermute | solution.py:19
  397.0 7.7 %collective-permute-start.3 = (f32[2,128,128]{2,1,0:T(8,128)S(1)}, f32[2,128,128]{2,1,0:T(8,128)S(1)}, u32[]{:S(2)}, u32[]{:S(2)}) collective-permute-start(f32[2,128,128]{2,1,0:T(8,128)S(1)} %get-tuple-element.533), channel_id=1, source_target_pairs={{1,0},{2,1},{3,2},{4,3},{5,4},{6,5},{7,6},{8,7},{9,8},{10,9},{11,1... | collective-permute-start | bytes 393224 | tf_op jit(solution)/shard_map/while/body/eval_jaxpr/ppermute | solution.py:19
  415.2 7.7 %collective-permute-start.3 = (f32[2,128,128]{2,1,0:T(8,128)S(1)}, f32[2,128,128]{2,1,0:T(8,128)S(1)}, u32[]{:S(2)}, u32[]{:S(2)}) collective-permute-start(f32[2,128,128]{2,1,0:T(8,128)S(1)} %get-tuple-element.533), channel_id=1, source_target_pairs={{1,0},{2,1},{3,2},{4,3},{5,4},{6,5},{7,6},{8,7},{9,8},{10,9},{11,1... | collective-permute-start | bytes 393224 | tf_op jit(solution)/shard_map/while/body/eval_jaxpr/ppermute | solution.py:19
  433.5 7.7 %collective-permute-start.3 = (f32[2,128,128]{2,1,0:T(8,128)S(1)}, f32[2,128,128]{2,1,0:T(8,128)S(1)}, u32[]{:S(2)}, u32[]{:S(2)}) collective-permute-start(f32[2,128,128]{2,1,0:T(8,128)S(1)} %get-tuple-element.533), channel_id=1, source_target_pairs={{1,0},{2,1},{3,2},{4,3},{5,4},{6,5},{7,6},{8,7},{9,8},{10,9},{11,1... | collective-permute-start | bytes 393224 | tf_op jit(solution)/shard_map/while/body/eval_jaxpr/ppermute | solution.py:19
  451.7 7.7 %collective-permute-start.3 = (f32[2,128,128]{2,1,0:T(8,128)S(1)}, f32[2,128,128]{2,1,0:T(8,128)S(1)}, u32[]{:S(2)}, u32[]{:S(2)}) collective-permute-start(f32[2,128,128]{2,1,0:T(8,128)S(1)} %get-tuple-element.533), channel_id=1, source_target_pairs={{1,0},{2,1},{3,2},{4,3},{5,4},{6,5},{7,6},{8,7},{9,8},{10,9},{11,1... | collective-permute-start | bytes 393224 | tf_op jit(solution)/shard_map/while/body/eval_jaxpr/ppermute | solution.py:19
  469.9 7.6 %collective-permute-start.3 = (f32[2,128,128]{2,1,0:T(8,128)S(1)}, f32[2,128,128]{2,1,0:T(8,128)S(1)}, u32[]{:S(2)}, u32[]{:S(2)}) collective-permute-start(f32[2,128,128]{2,1,0:T(8,128)S(1)} %get-tuple-element.533), channel_id=1, source_target_pairs={{1,0},{2,1},{3,2},{4,3},{5,4},{6,5},{7,6},{8,7},{9,8},{10,9},{11,1... | collective-permute-start | bytes 393224 | tf_op jit(solution)/shard_map/while/body/eval_jaxpr/ppermute | solution.py:19
  488.0 7.5 %collective-permute-start.3 = (f32[2,128,128]{2,1,0:T(8,128)S(1)}, f32[2,128,128]{2,1,0:T(8,128)S(1)}, u32[]{:S(2)}, u32[]{:S(2)}) collective-permute-start(f32[2,128,128]{2,1,0:T(8,128)S(1)} %get-tuple-element.533), channel_id=1, source_target_pairs={{1,0},{2,1},{3,2},{4,3},{5,4},{6,5},{7,6},{8,7},{9,8},{10,9},{11,1... | collective-permute-start | bytes 393224 | tf_op jit(solution)/shard_map/while/body/eval_jaxpr/ppermute | solution.py:19
  (52 other events, 2038.3 us)
where the time goes:
time: 710 us; the launch traced here: 700 us
  local copies, waits for them, and re-layouts  231 us (33%)
  other arithmetic  154 us (22%)
  starting transfers between devices  139 us (20%)
  waiting for transfers between devices  82.2 us (12%)
  blocking collectives  65.1 us (9%)
  matrix products  23.5 us (3%)
    another operation x28, local copies, waits for them, and re-layouts, lifting(): jnp.stack([padded[a:a + planes, b:b + rows_y, c:c + rows_z] for a, b, c i...  100 us
    ppermute x25, starting transfers between devices, padded_2(): lax.ppermute(head, axis, [((i + 1) % count, i) for i in range(ends)])  87.4 us
    scatter-add x24, other arithmetic, inject(): field.reshape(-1).at[clipped].add(jnp.where(inside, values, 0.0))  87.1 us
    ppermute x25, waiting for transfers between devices, padded_2(): lax.ppermute(head, axis, [((i + 1) % count, i) for i in range(ends)])  82.1 us
    gather x12, local copies, waits for them, and re-layouts, sample(): return jnp.where(inside, field.reshape(-1)[clipped], 0.0)  73.7 us
    ppermute x25, starting transfers between devices, padded_2(): lax.ppermute(tail, axis, [(i, (i + 1) % count) for i in range(ends)])  51.5 us
    psum x1, blocking collectives, per_device(): residual_traces = lax.psum(records, 'gx') - observed  45.2 us
    unnamed x33, local copies, waits for them, and re-layouts  29.3 us
  transfers between devices with their start and end apart: 50, of which 25 were waited for; matrix products, arithmetic and copies ran while one was open for 2% of the time, Pallas kernels for 0%

commit v1 on v0

--- a/solution.py
+++ b/solution.py
@@ -127,7 +127,7 @@
         )
 
     _, (changes, records) = lax.scan(forward_step, (wave_prev, wave_now), wavelet)
-    residual_traces = lax.psum(records, "gx") - observed
+    residual_traces = jnp.sum(lax.all_gather(records, "gx"), axis=0) - observed
     zeros_field = jnp.zeros(field_shape, jnp.float32)
 
     def adjoint_step(loop_state, inputs):

time: 710 us -> 683 us (0.962)
  blocking collectives: 65.1 us -> 41.9 us
  starting transfers between devices: 139 us -> 117 us
  waiting for transfers between devices: 82.2 us -> 99 us
    psum x1 -> x0, blocking collectives: 45.2 us -> none  [per_device(): residual_traces = lax.psum(records, 'gx') - observed]
    all_gather x0 -> x1, blocking collectives: none -> 21.9 us  [per_device(): residual_traces = jnp.sum(lax.all_gather(records, 'gx'), axis=0) - observed]
    ppermute x25, starting transfers between devices: 87.4 us -> 66.7 us  [padded_2(): lax.ppermute(head, axis, [((i + 1) % count, i) for i in range(ends)])]
    ppermute x25, waiting for transfers between devices: 82.1 us -> 98.9 us  [padded_2(): lax.ppermute(head, axis, [((i + 1) % count, i) for i in range(ends)])]
where the time goes in v1:
time: 683 us; the launch traced here: 673 us
  local copies, waits for them, and re-layouts  231 us (34%)
  other arithmetic  156 us (23%)
  starting transfers between devices  117 us (17%)
  waiting for transfers between devices  99 us (14%)
  blocking collectives  41.9 us (6%)
  matrix products  23.5 us (3%)
    another operation x28, local copies, waits for them, and re-layouts, lifting(): jnp.stack([padded[a:a + planes, b:b + rows_y, c:c + rows_z] for a, b, c i...  100 us
    ppermute x25, waiting for transfers between devices, padded_2(): lax.ppermute(head, axis, [((i + 1) % count, i) for i in range(ends)])  98.9 us
    scatter-add x24, other arithmetic, inject(): field.reshape(-1).at[clipped].add(jnp.where(inside, values, 0.0))  87.1 us
    gather x12, local copies, waits for them, and re-layouts, sample(): return jnp.where(inside, field.reshape(-1)[clipped], 0.0)  73.7 us
    ppermute x25, starting transfers between devices, padded_2(): lax.ppermute(head, axis, [((i + 1) % count, i) for i in range(ends)])  66.7 us
    ppermute x25, starting transfers between devices, padded_2(): lax.ppermute(tail, axis, [(i, (i + 1) % count) for i in range(ends)])  50.4 us
    unnamed x33, local copies, waits for them, and re-layouts  29.3 us
    add x24, other arithmetic, leapfrog(): return 2.0 * widened[2:-2] - before + coeffs * laplace(widened)  28.2 us
  transfers between devices with their start and end apart: 50, of which 25 were waited for; matrix products, arithmetic and copies ran while one was open for 2% of the time, Pallas kernels for 0%

profile of v1, /device:TPU:11, one launch (start us, length us, event | category | flops | bytes accessed | tf_op | source)
XLA Modules:
  0.0 673.3 jit_solution(1738072544071825721)
XLA Ops:
  3.5 228.7 %while.36 = (s32[]{:T(128)}, f32[8,128,128]{2,1,0:T(8,128)S(1)}, f32[8,128,128]{2,1,0:T(8,128)S(1)}, f32[12,8,128,128]{3,2,1,0:T(8,128)}, f32[12,1024]{1,0:T(8,1...) while((s32[]{:T(128)}, f32[8,128,128]{2,1,0:T(8,128)S(1)}, ...), condition=%wide.region_1.2_spmd, body=%wide.region_0.1_spmd.sunk | while | flops 3156997 | bytes 12133655 | solution.py:129
  34.9 6.1 gather_fusion
  232.2 21.9 %all-gather.1 = f32[16,12,1024]{2,1,0:T(8,128)} all-gather(f32[1,12,1024]{2,1,0:T(8,128)S(1)} %bitcast.216), channel_id=2, replica_groups=mesh['shots'=2,'gx'=16] {'gx'}, dimensions={0}, use_global_device_ids=true | all-gather | bytes 835584 | tf_op jit(solution)/shard_map/all_gather | solution.py:130
  255.7 6.2 rev.7
  262.0 215.1 %while.37 = (s32[]{:T(128)}, f32[8,128,128]{2,1,0:T(8,128)S(1)}, f32[8,128,128]{2,1,0:T(8,128)S(1)}, f32[8,128,128]{2,1,0:T(8,128)S(1)}, f32[8,128,128]{2,1,0:T(...) while((s32[]{:T(128)}, f32[8,128,128]{2,1,0:T(8,128)S(1)}, ...), condition=%wide.region_6.7_spmd.clone, body=%wide.region_4.6_spmd.clone.sunk | while | flops 3156995 | bytes 12112095 | solution.py:139
  271.5 6.4 scatter_fusion
  288.9 6.4 scatter_fusion
  306.9 6.4 scatter_fusion
  324.9 6.4 scatter_fusion
  343.0 6.4 scatter_fusion
  361.0 6.4 scatter_fusion
  379.1 6.4 scatter_fusion
  397.1 6.4 scatter_fusion
  415.2 6.4 scatter_fusion
  433.2 6.4 scatter_fusion
  451.2 6.4 scatter_fusion
  469.3 6.4 scatter_fusion
  536.8 54.1 %stack.111 = bf16[27,163840]{1,0:T(8,128)(2,1)} concatenate(bf16[1,163840]{1,0:T(2,128)(2,1)} %stack.84, bf16[1,163840]{1,0:T(2,128)(2,1)} %stack.85, bf16[1,163840]{1,0:T(2,128)(2,1)} %stack.86, bf16[1,163840]{1,0:T(2,128)(2,1)} %stack.87, bf16[1,163840]{1,0:T(2,128)(2,1)S(1)} %stack.88, bf16[1,163840]{1,0:T(2,128)(2,1)} %stack.89, bf16[1,163840]{1,0:T(2,128)(2,1)} %stack.90, ...), dimensions={0} | concatenate | bytes 17694720 | tf_op jit(solution)/shard_map/stack | solution.py:64
  590.9 10.8 %fusion.31 = bf16[163840,32]{0,1:T(8,128)(2,1)} fusion(bf16[27,163840]{1,0:T(8,128)(2,1)} %stack.111, bf16[32,27]{1,0:T(8,128)(2,1)S(1)} %copy-done, f32[32]{0:T(128)S(1)} %copy-done.12), kind=kOutput, calls=%fused_computation.95 | convolution fusion | flops 298844160 | bytes 19334976 | tf_op jit(solution)/shard_map/dot_general | solution.py:67
  601.9 12.7 %fusion.35 = f32[163840,27]{0,1:T(8,128)} fusion(bf16[27,32]{1,0:T(8,128)(2,1)S(1)} %copy-done.10, bf16[32,32]{1,0:T(8,128)(2,1)S(1)} %copy-done.9, bf16[163840,32]{0,1:T(8,128)(2,1)} %fusion.31, f32[32]{0:T(128)S(1)} %copy-done.11, pred[163840]{0:T(1024)(128)(4,1)S(1)} %bitcast.209), kind=kOutput, calls=%fused_computation.99 | convolution fusion | flops 639631360 | bytes 28348224 | tf_op jit(solution)/shard_map/dot_general | solution.py:78
  614.6 19.2 %copy.24 = f32[4,8,1280,128]{3,2,1,0:T(8,128)} copy(f32[4,8,1280,128]{3,1,2,0:T(8,128)} %bitcast.205) | data formatting | bytes 41943040
  633.9 7.1 %slice.443 = f32[27,1280,128]{2,1,0:T(8,128)S(1)} slice(f32[32,1280,128]{2,1,0:T(8,128)} %bitcast.207), slice={[0:27], [0:1280], [0:128]} | slice | bytes 35389440
  643.6 9.0 %scatter_fusion.1 = bf16[16,16,1024]{2,1,0:T(8,128)(2,1)S(1)} fusion(bf16[16,16,1024]{2,1,0:T(8,128)(2,1)S(1)} %broadcast_in_dim.77, s32[128]{0:T(128)S(1)} %fusion.78, bf16[128,1024]{1,0:T(8,128)(2,1)S(1)} %bitcast_select_fusion), kind=kCustom, calls=%fused_computation.2 | custom fusion | bytes 787456 | tf_op jit(solution)/shard_map/scatter | solution.py:163
  652.5 20.0 %all_to_all.5 = bf16[16,16,1024]{2,1,0:T(8,128)(2,1)S(1)} all-to-all(bf16[16,16,1024]{2,1,0:T(8,128)(2,1)S(1)} %scatter_fusion.1), channel_id=1, replica_groups=mesh['shots'=2,'gx'=16] {'gx'}, dimensions={0} | all-to-all | bytes 1048576 | tf_op jit(solution)/shard_map/all_to_all | solution.py:165
  (524 shorter events, 423.7 us)
Async XLA Ops:
  3.5 6.4 collective-permute-start
  7.2 6.3 collective-permute-start.1
  25.3 7.1 %collective-permute-start.1 = (f32[2,128,128]{2,1,0:T(8,128)S(1)}, f32[2,128,128]{2,1,0:T(8,128)S(1)}, u32[]{:S(2)}, u32[]{:S(2)}) collective-permute-start(f32[2,128,128]{2,1,0:T(8,128)S(1)} %get-tuple-element.520), channel_id=1, source_target_pairs={{1,0},{2,1},{3,2},{4,3},{5,4},{6,5},{7,6},{8,7},{9,8},{10,9},{11,1... | collective-permute-start | bytes 393224 | tf_op jit(solution)/shard_map/while/body/eval_jaxpr/ppermute | solution.py:19
  44.2 7.2 %collective-permute-start.1 = (f32[2,128,128]{2,1,0:T(8,128)S(1)}, f32[2,128,128]{2,1,0:T(8,128)S(1)}, u32[]{:S(2)}, u32[]{:S(2)}) collective-permute-start(f32[2,128,128]{2,1,0:T(8,128)S(1)} %get-tuple-element.520), channel_id=1, source_target_pairs={{1,0},{2,1},{3,2},{4,3},{5,4},{6,5},{7,6},{8,7},{9,8},{10,9},{11,1... | collective-permute-start | bytes 393224 | tf_op jit(solution)/shard_map/while/body/eval_jaxpr/ppermute | solution.py:19
  63.2 7.2 %collective-permute-start.1 = (f32[2,128,128]{2,1,0:T(8,128)S(1)}, f32[2,128,128]{2,1,0:T(8,128)S(1)}, u32[]{:S(2)}, u32[]{:S(2)}) collective-permute-start(f32[2,128,128]{2,1,0:T(8,128)S(1)} %get-tuple-element.520), channel_id=1, source_target_pairs={{1,0},{2,1},{3,2},{4,3},{5,4},{6,5},{7,6},{8,7},{9,8},{10,9},{11,1... | collective-permute-start | bytes 393224 | tf_op jit(solution)/shard_map/while/body/eval_jaxpr/ppermute | solution.py:19
  82.2 7.2 %collective-permute-start.1 = (f32[2,128,128]{2,1,0:T(8,128)S(1)}, f32[2,128,128]{2,1,0:T(8,128)S(1)}, u32[]{:S(2)}, u32[]{:S(2)}) collective-permute-start(f32[2,128,128]{2,1,0:T(8,128)S(1)} %get-tuple-element.520), channel_id=1, source_target_pairs={{1,0},{2,1},{3,2},{4,3},{5,4},{6,5},{7,6},{8,7},{9,8},{10,9},{11,1... | collective-permute-start | bytes 393224 | tf_op jit(solution)/shard_map/while/body/eval_jaxpr/ppermute | solution.py:19
  101.2 7.2 %collective-permute-start.1 = (f32[2,128,128]{2,1,0:T(8,128)S(1)}, f32[2,128,128]{2,1,0:T(8,128)S(1)}, u32[]{:S(2)}, u32[]{:S(2)}) collective-permute-start(f32[2,128,128]{2,1,0:T(8,128)S(1)} %get-tuple-element.520), channel_id=1, source_target_pairs={{1,0},{2,1},{3,2},{4,3},{5,4},{6,5},{7,6},{8,7},{9,8},{10,9},{11,1... | collective-permute-start | bytes 393224 | tf_op jit(solution)/shard_map/while/body/eval_jaxpr/ppermute | solution.py:19
  120.2 7.2 %collective-permute-start.1 = (f32[2,128,128]{2,1,0:T(8,128)S(1)}, f32[2,128,128]{2,1,0:T(8,128)S(1)}, u32[]{:S(2)}, u32[]{:S(2)}) collective-permute-start(f32[2,128,128]{2,1,0:T(8,128)S(1)} %get-tuple-element.520), channel_id=1, source_target_pairs={{1,0},{2,1},{3,2},{4,3},{5,4},{6,5},{7,6},{8,7},{9,8},{10,9},{11,1... | collective-permute-start | bytes 393224 | tf_op jit(solution)/shard_map/while/body/eval_jaxpr/ppermute | solution.py:19
  139.2 7.2 %collective-permute-start.1 = (f32[2,128,128]{2,1,0:T(8,128)S(1)}, f32[2,128,128]{2,1,0:T(8,128)S(1)}, u32[]{:S(2)}, u32[]{:S(2)}) collective-permute-start(f32[2,128,128]{2,1,0:T(8,128)S(1)} %get-tuple-element.520), channel_id=1, source_target_pairs={{1,0},{2,1},{3,2},{4,3},{5,4},{6,5},{7,6},{8,7},{9,8},{10,9},{11,1... | collective-permute-start | bytes 393224 | tf_op jit(solution)/shard_map/while/body/eval_jaxpr/ppermute | solution.py:19
  158.2 7.2 %collective-permute-start.1 = (f32[2,128,128]{2,1,0:T(8,128)S(1)}, f32[2,128,128]{2,1,0:T(8,128)S(1)}, u32[]{:S(2)}, u32[]{:S(2)}) collective-permute-start(f32[2,128,128]{2,1,0:T(8,128)S(1)} %get-tuple-element.520), channel_id=1, source_target_pairs={{1,0},{2,1},{3,2},{4,3},{5,4},{6,5},{7,6},{8,7},{9,8},{10,9},{11,1... | collective-permute-start | bytes 393224 | tf_op jit(solution)/shard_map/while/body/eval_jaxpr/ppermute | solution.py:19
  177.2 7.2 %collective-permute-start.1 = (f32[2,128,128]{2,1,0:T(8,128)S(1)}, f32[2,128,128]{2,1,0:T(8,128)S(1)}, u32[]{:S(2)}, u32[]{:S(2)}) collective-permute-start(f32[2,128,128]{2,1,0:T(8,128)S(1)} %get-tuple-element.520), channel_id=1, source_target_pairs={{1,0},{2,1},{3,2},{4,3},{5,4},{6,5},{7,6},{8,7},{9,8},{10,9},{11,1... | collective-permute-start | bytes 393224 | tf_op jit(solution)/shard_map/while/body/eval_jaxpr/ppermute | solution.py:19
  196.2 7.2 %collective-permute-start.1 = (f32[2,128,128]{2,1,0:T(8,128)S(1)}, f32[2,128,128]{2,1,0:T(8,128)S(1)}, u32[]{:S(2)}, u32[]{:S(2)}) collective-permute-start(f32[2,128,128]{2,1,0:T(8,128)S(1)} %get-tuple-element.520), channel_id=1, source_target_pairs={{1,0},{2,1},{3,2},{4,3},{5,4},{6,5},{7,6},{8,7},{9,8},{10,9},{11,1... | collective-permute-start | bytes 393224 | tf_op jit(solution)/shard_map/while/body/eval_jaxpr/ppermute | solution.py:19
  215.1 7.2 %collective-permute-start.1 = (f32[2,128,128]{2,1,0:T(8,128)S(1)}, f32[2,128,128]{2,1,0:T(8,128)S(1)}, u32[]{:S(2)}, u32[]{:S(2)}) collective-permute-start(f32[2,128,128]{2,1,0:T(8,128)S(1)} %get-tuple-element.520), channel_id=1, source_target_pairs={{1,0},{2,1},{3,2},{4,3},{5,4},{6,5},{7,6},{8,7},{9,8},{10,9},{11,1... | collective-permute-start | bytes 393224 | tf_op jit(solution)/shard_map/while/body/eval_jaxpr/ppermute | solution.py:19
  281.3 6.8 %collective-permute-start.3 = (f32[2,128,128]{2,1,0:T(8,128)S(1)}, f32[2,128,128]{2,1,0:T(8,128)S(1)}, u32[]{:S(2)}, u32[]{:S(2)}) collective-permute-start(f32[2,128,128]{2,1,0:T(8,128)S(1)} %get-tuple-element.533), channel_id=1, source_target_pairs={{1,0},{2,1},{3,2},{4,3},{5,4},{6,5},{7,6},{8,7},{9,8},{10,9},{11,1... | collective-permute-start | bytes 393224 | tf_op jit(solution)/shard_map/while/body/eval_jaxpr/ppermute | solution.py:19
  298.7 7.5 %collective-permute-start.3 = (f32[2,128,128]{2,1,0:T(8,128)S(1)}, f32[2,128,128]{2,1,0:T(8,128)S(1)}, u32[]{:S(2)}, u32[]{:S(2)}) collective-permute-start(f32[2,128,128]{2,1,0:T(8,128)S(1)} %get-tuple-element.533), channel_id=1, source_target_pairs={{1,0},{2,1},{3,2},{4,3},{5,4},{6,5},{7,6},{8,7},{9,8},{10,9},{11,1... | collective-permute-start | bytes 393224 | tf_op jit(solution)/shard_map/while/body/eval_jaxpr/ppermute | solution.py:19
  316.7 7.5 %collective-permute-start.3 = (f32[2,128,128]{2,1,0:T(8,128)S(1)}, f32[2,128,128]{2,1,0:T(8,128)S(1)}, u32[]{:S(2)}, u32[]{:S(2)}) collective-permute-start(f32[2,128,128]{2,1,0:T(8,128)S(1)} %get-tuple-element.533), channel_id=1, source_target_pairs={{1,0},{2,1},{3,2},{4,3},{5,4},{6,5},{7,6},{8,7},{9,8},{10,9},{11,1... | collective-permute-start | bytes 393224 | tf_op jit(solution)/shard_map/while/body/eval_jaxpr/ppermute | solution.py:19
  334.7 7.5 %collective-permute-start.3 = (f32[2,128,128]{2,1,0:T(8,128)S(1)}, f32[2,128,128]{2,1,0:T(8,128)S(1)}, u32[]{:S(2)}, u32[]{:S(2)}) collective-permute-start(f32[2,128,128]{2,1,0:T(8,128)S(1)} %get-tuple-element.533), channel_id=1, source_target_pairs={{1,0},{2,1},{3,2},{4,3},{5,4},{6,5},{7,6},{8,7},{9,8},{10,9},{11,1... | collective-permute-start | bytes 393224 | tf_op jit(solution)/shard_map/while/body/eval_jaxpr/ppermute | solution.py:19
  352.8 7.5 %collective-permute-start.3 = (f32[2,128,128]{2,1,0:T(8,128)S(1)}, f32[2,128,128]{2,1,0:T(8,128)S(1)}, u32[]{:S(2)}, u32[]{:S(2)}) collective-permute-start(f32[2,128,128]{2,1,0:T(8,128)S(1)} %get-tuple-element.533), channel_id=1, source_target_pairs={{1,0},{2,1},{3,2},{4,3},{5,4},{6,5},{7,6},{8,7},{9,8},{10,9},{11,1... | collective-permute-start | bytes 393224 | tf_op jit(solution)/shard_map/while/body/eval_jaxpr/ppermute | solution.py:19
  370.8 7.5 %collective-permute-start.3 = (f32[2,128,128]{2,1,0:T(8,128)S(1)}, f32[2,128,128]{2,1,0:T(8,128)S(1)}, u32[]{:S(2)}, u32[]{:S(2)}) collective-permute-start(f32[2,128,128]{2,1,0:T(8,128)S(1)} %get-tuple-element.533), channel_id=1, source_target_pairs={{1,0},{2,1},{3,2},{4,3},{5,4},{6,5},{7,6},{8,7},{9,8},{10,9},{11,1... | collective-permute-start | bytes 393224 | tf_op jit(solution)/shard_map/while/body/eval_jaxpr/ppermute | solution.py:19
  388.9 7.5 %collective-permute-start.3 = (f32[2,128,128]{2,1,0:T(8,128)S(1)}, f32[2,128,128]{2,1,0:T(8,128)S(1)}, u32[]{:S(2)}, u32[]{:S(2)}) collective-permute-start(f32[2,128,128]{2,1,0:T(8,128)S(1)} %get-tuple-element.533), channel_id=1, source_target_pairs={{1,0},{2,1},{3,2},{4,3},{5,4},{6,5},{7,6},{8,7},{9,8},{10,9},{11,1... | collective-permute-start | bytes 393224 | tf_op jit(solution)/shard_map/while/body/eval_jaxpr/ppermute | solution.py:19
  406.9 7.5 %collective-permute-start.3 = (f32[2,128,128]{2,1,0:T(8,128)S(1)}, f32[2,128,128]{2,1,0:T(8,128)S(1)}, u32[]{:S(2)}, u32[]{:S(2)}) collective-permute-start(f32[2,128,128]{2,1,0:T(8,128)S(1)} %get-tuple-element.533), channel_id=1, source_target_pairs={{1,0},{2,1},{3,2},{4,3},{5,4},{6,5},{7,6},{8,7},{9,8},{10,9},{11,1... | collective-permute-start | bytes 393224 | tf_op jit(solution)/shard_map/while/body/eval_jaxpr/ppermute | solution.py:19
  425.0 7.5 %collective-permute-start.3 = (f32[2,128,128]{2,1,0:T(8,128)S(1)}, f32[2,128,128]{2,1,0:T(8,128)S(1)}, u32[]{:S(2)}, u32[]{:S(2)}) collective-permute-start(f32[2,128,128]{2,1,0:T(8,128)S(1)} %get-tuple-element.533), channel_id=1, source_target_pairs={{1,0},{2,1},{3,2},{4,3},{5,4},{6,5},{7,6},{8,7},{9,8},{10,9},{11,1... | collective-permute-start | bytes 393224 | tf_op jit(solution)/shard_map/while/body/eval_jaxpr/ppermute | solution.py:19
  443.0 7.5 %collective-permute-start.3 = (f32[2,128,128]{2,1,0:T(8,128)S(1)}, f32[2,128,128]{2,1,0:T(8,128)S(1)}, u32[]{:S(2)}, u32[]{:S(2)}) collective-permute-start(f32[2,128,128]{2,1,0:T(8,128)S(1)} %get-tuple-element.533), channel_id=1, source_target_pairs={{1,0},{2,1},{3,2},{4,3},{5,4},{6,5},{7,6},{8,7},{9,8},{10,9},{11,1... | collective-permute-start | bytes 393224 | tf_op jit(solution)/shard_map/while/body/eval_jaxpr/ppermute | solution.py:19
  461.1 7.5 %collective-permute-start.3 = (f32[2,128,128]{2,1,0:T(8,128)S(1)}, f32[2,128,128]{2,1,0:T(8,128)S(1)}, u32[]{:S(2)}, u32[]{:S(2)}) collective-permute-start(f32[2,128,128]{2,1,0:T(8,128)S(1)} %get-tuple-element.533), channel_id=1, source_target_pairs={{1,0},{2,1},{3,2},{4,3},{5,4},{6,5},{7,6},{8,7},{9,8},{10,9},{11,1... | collective-permute-start | bytes 393224 | tf_op jit(solution)/shard_map/while/body/eval_jaxpr/ppermute | solution.py:19
  (52 other events, 1878.5 us)
